TPU v7x, 32 devices: a whole 2x2x4 slice. The times are simulated.
32 devices in a mesh: groups: 2 (over y), fsdp: 8 (over z, x), dp: 2 (over core).
Axes of the slice: x: 2, y: 2, z: 4, core: 2. Of those that a mesh axis runs over, the one named last changes fastest.
Arguments:
- acts: bfloat16 [2, 32, 128, 14336], P(None, ('groups', 'fsdp', 'dp')), parts along dimension 1, may hold values from -48 to 48
- grads_out: bfloat16 [2, 32, 128, 4096], P(None, ('groups', 'fsdp', 'dp')), parts along dimension 1, may hold values from -48 to 48
- basis_in: bfloat16 [2, 14336, 64], P(None, 'fsdp'), may hold values from -0.046875 to 0.046875
- basis_out: bfloat16 [2, 4096, 64], P(None, 'fsdp'), may hold values from -0.09375 to 0.09375
- query_codes: bfloat16 [1024, 8192], P(('fsdp', 'dp')), may hold values from -6 to 6
Outputs:
- scores: float32 [32, 1024], P(('groups', 'fsdp', 'dp')), parts along dimension 0
There are 2 independent parts, one for each index of `groups`. A program takes and returns all parts, laid end to end along the dimension named above; an argument that names none is the same for every part. Nothing has to cross between parts.
All inputs are finite; a program needn't handle non-finite values.
Results may differ from a plain program's by a relative error of at most 0.0003.
Values may be sent and summed in bfloat16 or wider, within the bound.
A program may use at most 128 MiB of HBM per device.

v0:
```python
import math

import jax
import jax.numpy as jnp
from jax import lax
from jax.sharding import PartitionSpec as P


def damped_inverse(covariance, samples):
    averaged = covariance / samples
    ridge_term = 0.1 * jnp.trace(averaged) / averaged.shape[0]
    identity_matrix = jnp.eye(averaged.shape[0], dtype=averaged.dtype)
    factor = jnp.linalg.cholesky(averaged + ridge_term * identity_matrix)
    return jax.scipy.linalg.cho_solve((factor, True), identity_matrix)


def condition(blocks, inverse_in, output_inverse):
    highest_precision = lax.Precision.HIGHEST
    middle_product = jnp.einsum("lij,eljk->elik", inverse_in, blocks, precision=highest_precision)
    return jnp.einsum("bzpo,zoc->bzpc", middle_product, output_inverse, precision=highest_precision)


def projector(source, block_rows):
    return jnp.einsum("ltf,lfr->ltr", source, block_rows, preferred_element_type=jnp.float32)


def inner_row_count(left_rows, right_rows):
    return lax.dot_general(
        left_rows, right_rows, (((1,), (1,)), ((), ())), precision=lax.Precision.HIGHEST
    )


def on_device(acts, grads_out, basis_in, basis_out, query_codes):
    layers, sequences, length, hidden_width = acts.shape
    model_width = grads_out.shape[3]
    code_rank = basis_in.shape[2]
    tok_rows = sequences * length
    code_width = layers * code_rank * code_rank
    highest_precision = lax.Precision.HIGHEST
    flat_acts = acts.reshape(layers, tok_rows, hidden_width)
    flattened_gradients = grads_out.reshape(layers, tok_rows, model_width)
    projected_in = projector(flat_acts, lax.all_gather(basis_in, "fsdp", axis=1, tiled=True))
    projected_out = projector(
        flattened_gradients, lax.all_gather(basis_out, "fsdp", axis=1, tiled=True)
    )
    covariance_in = jnp.einsum(
        "lti,ltj->lij", projected_in, projected_in, precision=highest_precision
    )
    covariance_out = jnp.einsum(
        "lti,ltj->lij", projected_out, projected_out, precision=highest_precision
    )
    shaped_in = projected_in.reshape(layers, sequences, length, code_rank)
    shaped_out = projected_out.reshape(layers, sequences, length, code_rank)
    gradient_codes = jnp.einsum(
        "lsti,lstj->slij", shaped_in, shaped_out, precision=highest_precision
    )
    covariance_in, covariance_out = lax.psum((covariance_in, covariance_out), ("fsdp", "dp"))
    samples = float(sequences * lax.axis_size(("fsdp", "dp")) * length)
    inverse_in = jax.vmap(damped_inverse, in_axes=(0, None))(covariance_in, samples)
    output_inverse = jax.vmap(damped_inverse, in_axes=(0, None))(covariance_out, samples)
    factor_scale = 1.0 / math.sqrt(code_width * length)
    local_codes = condition(gradient_codes, inverse_in, output_inverse).reshape(
        sequences, code_width
    )
    return (
        inner_row_count(
            local_codes,
            lax.all_gather(query_codes, ("fsdp", "dp"), axis=0, tiled=True).astype(jnp.float32),
        )
        * factor_scale
    )


def solution(mesh):
    placed = (
        P(None, ("groups", "fsdp", "dp"), None, None),
        P(None, ("groups", "fsdp", "dp"), None, None),
        P(None, "fsdp", None),
        P(None, "fsdp", None),
        P(("fsdp", "dp"), None),
    )
    return jax.shard_map(
        on_device,
        mesh=mesh,
        in_specs=placed,
        out_specs=P(("groups", "fsdp", "dp"), None),
        check_vma=False,
    )
```

profile of v0, /device:TPU:0, one launch (start us, length us, event | category | flops | bytes accessed | tf_op | source)
XLA Modules:
  0.0 367.7 jit_solution(14522161505544894561)
XLA Ops:
  6.5 0.7 all-gather.4.cloned.1.call-update
  7.3 0.7 all-gather.6.cloned.1.call-update
  8.1 43.6 %all-gather.4.cloned.1.call-done = bf16[2,4096,64]{1,2,0:T(8,128)(2,1)} async-done(((bf16[2,512,64]{1,2,0:T(8,128)(2,1)}), bf16[2,4096,64]{1,2,0:T(8,128)(2,1)}) %all-gather.4.cloned.1.call-update) | async-done | bytes 1048592 | tf_op jit(solution)/shard_map/all_gather | solution.py:44
  51.7 2.1 fusion.2
  53.7 0.9 fusion.17
  54.6 64.9 %all-gather.6.cloned.1.call-done = bf16[2,14336,64]{1,2,0:T(8,128)(2,1)} async-done(((bf16[2,1792,64]{1,2,0:T(8,128)(2,1)}), bf16[2,14336,64]{1,2,0:T(8,128)(2,1)}) %all-gather.6.cloned.1.call-update) | async-done | bytes 3670032 | tf_op jit(solution)/shard_map/all_gather | solution.py:42
  119.5 6.8 %fusion = f32[2,128,64]{1,2,0:T(8,128)S(1)} fusion(bf16[2,14336,64]{1,2,0:T(8,128)(2,1)} %all-gather.6.cloned.1.call-done, bf16[2,1,128,14336]{3,2,1,0:T(8,128)(2,1)} %param.8), kind=kOutput, calls=%fused_computation | convolution fusion | flops 469762048 | bytes 11075584 | tf_op jit(solution)/shard_map/ltf,lfr->ltr/dot_general | solution.py:24
  126.3 0.9 fusion.19
  127.3 0.5 all-gather.8.cloned.1.call-update
  127.9 0.2 fusion.18
  128.2 84.9 %all-reduce.3.cloned.1.call-done = (f32[2,64,64]{1,2,0:T(8,128)}, f32[2,64,64]{1,2,0:T(8,128)}) async-done(((f32[2,64,64]{1,2,0:T(8,128)}, f32[2,64,64]{1,2,0:T(8,128)}), (f32[2,64,64]{1,2,0:T(8,128)}, f32[2,64,64]{1,2,0:T(8,128)})) %all-reduce.3.cloned.1.call-update) | async-done | bytes 65552 | tf_op jit(solution)/shard_map/psum | solution.py:57
  213.0 1.0 select_reduce_fusion.2
  214.0 1.0 multiply_add_fusion
  215.1 11.7 %custom-call.10 = f32[2,64,64]{2,1,0:T(8,128)S(1)} custom-call(f32[2,64,64]{2,1,0:T(8,128)S(1)} %fusion.13), custom_call_target="Cholesky" | custom-call | tf_op jit(solution)/shard_map/vmap(jit(cholesky))/cholesky | solution.py:13
  226.8 0.1 copy.26
  226.9 11.7 %custom-call.12 = f32[2,64,64]{2,1,0:T(8,128)S(1)} custom-call(f32[2,64,64]{2,1,0:T(8,128)S(1)} %fusion.8), custom_call_target="Cholesky" | custom-call | tf_op jit(solution)/shard_map/vmap(jit(cholesky))/cholesky | solution.py:13
  238.7 0.1 compare_reduce_fusion
  238.8 0.1 compare_reduce_fusion.1
  238.9 0.1 select_bitcast_fusion
  239.0 9.8 %custom-call.13 = f32[2,1,64,64]{2,3,1,0:T(8,128)S(1)} custom-call(f32[2,1,64,64]{3,2,1,0:T(8,128)S(1)} %get-tuple-element.15), custom_call_target="InvertDiagBlocksLowerTriangular" | custom-call | tf_op jit(solution)/shard_map/vmap(jit(_cho_solve))/triangular_solve | solution.py:14
  248.9 9.8 %custom-call.11 = f32[2,1,64,64]{2,3,1,0:T(8,128)S(1)} custom-call(f32[2,1,64,64]{3,2,1,0:T(8,128)S(1)} %get-tuple-element.16), custom_call_target="InvertDiagBlocksLowerTriangular" | custom-call | tf_op jit(solution)/shard_map/vmap(jit(_cho_solve))/triangular_solve | solution.py:14
  258.7 0.3 fusion.6
  259.0 0.3 fusion.11
  259.3 0.2 fusion.4
  259.5 0.3 fusion.9
  259.8 0.2 convolution_bitcast_fusion.1
  260.0 0.2 convolution_bitcast_fusion
  260.2 0.1 copy.32
  260.3 0.1 reshape.56
  260.4 83.6 %all-gather.8.cloned.1.call-done = bf16[1024,8192]{1,0:T(8,128)(2,1)} async-done(((bf16[64,8192]{1,0:T(8,128)(2,1)}), bf16[1024,8192]{1,0:T(8,128)(2,1)}) %all-gather.8.cloned.1.call-update) | async-done | bytes 16777232 | tf_op jit(solution)/shard_map/all_gather | solution.py:68
  344.0 16.5 %fusion.20 = f32[1,1024]{1,0:T(1,128)S(1)} fusion(f32[8192,1]{0,1:T(1,128)S(1)} %reshape.56, bf16[1024,8192]{1,0:T(8,128)(2,1)} %all-gather.8.cloned.1.call-done), kind=kOutput, calls=%fused_computation.40 | convolution fusion | flops 100663296 | bytes 16814080 | tf_op jit(solution)/shard_map/dot_general | solution.py:28
  360.6 0.6 broadcast_multiply_fusion
  (17 shorter events, 0.4 us)
Async XLA Ops:
  6.5 45.1 %copy-start = (bf16[2,1,128,4096]{3,2,1,0:T(8,128)(2,1)S(1)}, bf16[2,1,128,4096]{3,2,1,0:T(8,128)(2,1)}, u32[]{:S(2)}) copy-start(bf16[2,1,128,4096]{3,2,1,0:T(8,128)(2,1)} %param.9) | copy-start | bytes 6291460
  6.5 45.1 %all-gather.4.cloned.1.call-start = ((), (), s32[]{:S(2)}) async-start(), calls=%async_computation | async-start | bytes 1179648 | tf_op jit(solution)/shard_map/all_gather | solution.py:44
  7.3 112.2 %all-gather.6.cloned.1.call-start = ((), (), s32[]{:S(2)}) async-start(), calls=%async_computation.1 | async-start | bytes 4128768 | tf_op jit(solution)/shard_map/all_gather | solution.py:42
  8.0 205.0 %all-reduce.3.cloned.1.call-start = ((), (), s32[]{:S(2)}) async-start(), calls=%async_computation.3 | async-start | bytes 262144 | tf_op jit(solution)/shard_map/psum | solution.py:57
  127.2 216.8 %all-gather.8.cloned.1.call-start = ((), (), s32[]{:S(2)}) async-start(), calls=%async_computation.2 | async-start | bytes 17825792 | tf_op jit(solution)/shard_map/all_gather | solution.py:68
Sparse Core Ops, SparseCore 0:
  9.4 42.2 all-gather.3
  53.9 65.5 all-gather.5
  127.3 85.6 all-reduce.2
  215.1 128.9 all-gather.7
where the time goes:
time: 368 us
  waiting for transfers between devices  279 us (76%)
  other arithmetic  46.1 us (13%)
  matrix products  28.9 us (8%)
  between operations  13.3 us (4%)
    psum x1, waiting for transfers between devices, on_device(): lax.psum((covariance_in, covariance_out), ('fsdp', 'dp'))  84.9 us
    all_gather x1, waiting for transfers between devices, on_device(): lax.all_gather(query_codes, ('fsdp', 'dp'), axis=0, tiled=True)  83.6 us
    all_gather x1, waiting for transfers between devices, on_device(): lax.all_gather(basis_in, 'fsdp', axis=1, tiled=True)  64.9 us
    all_gather x1, waiting for transfers between devices, on_device(): lax.all_gather(basis_out, 'fsdp', axis=1, tiled=True)  43.6 us
    another operation x6, other arithmetic, damped_inverse(): factor = jnp.linalg.cholesky(averaged + ridge_term * identity_matrix)  23.7 us
    another operation x4, other arithmetic, damped_inverse(): return jax.scipy.linalg.cho_solve((factor, True), identity_matrix)  19.8 us
    dot_general x1, matrix products, inner_row_count(): lax.dot_general(left_rows, right_rows, (((1,), (1,)), ((), ())), precisio...  16.5 us
    dot_general x2, matrix products, projector(): jnp.einsum('ltf,lfr->ltr', source, block_rows, preferred_element_type=jnp...  8.91 us
  transfers between devices with their start and end apart: 4, of which 4 were waited for; matrix products, arithmetic and copies ran while one was open for 14% of the time, Pallas kernels for 0%

commit v1 on v0

v1 whole, which is shorter than its diff:
```python
import functools
import math

import jax
import jax.numpy as jnp
from jax import lax
from jax.experimental import pallas as pl
from jax.experimental.pallas import tpu as pltpu
from jax.sharding import PartitionSpec as P

MESH = pl.DeviceIdType.MESH
HIGHEST = lax.Precision.HIGHEST
F32 = jnp.float32


def dot(a, b, ca, cb, precision=None):
    return lax.dot_general(
        a, b, (((ca,), (cb,)), ((), ())), precision=precision, preferred_element_type=F32
    )


def invert_all(mats):
    n = mats[0].shape[0]
    rows = lax.broadcasted_iota(jnp.int32, (n, n), 0)
    lanes = lax.broadcasted_iota(jnp.int32, (n, n), 1)
    lane1 = lax.broadcasted_iota(jnp.int32, (1, n), 1)
    unit = jnp.where(rows == lanes, 1.0, 0.0).astype(F32)
    mats = list(mats)
    for k in range(n):
        for m, a in enumerate(mats):
            recip = 1.0 / a[k : k + 1, k : k + 1]
            col = a[:, k : k + 1]
            row = jnp.where(lane1 == k, 1.0, a[k : k + 1, :]) * recip
            cleared = jnp.where(lanes == k, unit, a)
            mats[m] = jnp.where(rows == k, row, cleared - col * row)
    return mats


def kernel(
    nf, nc, scale,
    acts_hbm, grads_hbm, basis_in, basis_out, query_hbm, out_ref,
    acts, grads, queries, win, wout, acc, arrived, codes, cond, flat, stage, landed,
    load_sem, bs_send, bs_recv, cov_send, cov_recv, g_send, g_recv, s_send, s_recv,
):
    f, c = lax.axis_index("fsdp"), lax.axis_index("dp")
    n = nf * nc
    bits = n.bit_length() - 1
    me = f * nc + c
    length = nf // 2
    z, x = f // 2, f % 2
    r = basis_in.shape[2]
    tokens = acts.shape[0] // 2

    loads = [
        pltpu.make_async_copy(src, dst, load_sem.at[i])
        for i, (src, dst) in enumerate(((grads_hbm, grads), (acts_hbm, acts), (query_hbm, queries)))
    ]
    for load in loads:
        load.start()

    def peer(rank):
        return {"fsdp": rank // nc, "dp": rank % nc}

    barrier = pltpu.get_barrier_semaphore()

    def greet(d, _):
        pl.semaphore_signal(barrier, inc=1, device_id=peer((me + d) % n), device_id_type=MESH)
        return _

    lax.fori_loop(1, n, greet, 0)

    kinds = ((win, basis_in), (wout, basis_out))
    for full, mine in kinds:
        rows = mine.shape[1]
        full[pl.ds(pl.multiple_of(f * rows, rows), rows), :] = jnp.concatenate(
            [mine[0], mine[1]], axis=1
        )
    pl.semaphore_wait(barrier, n - 1)

    def piece(kind, owner, half):
        full, mine = kinds[kind]
        rows = mine.shape[1] // 2
        return full.at[pl.ds(pl.multiple_of((owner * 2 + half) * rows, rows), rows), :]

    def hop(kind, owner, way):
        target = (f - 2, f + 2, f + 1 - 2 * x, f)[way]
        core = 1 - c if way == 3 else c
        return pltpu.make_async_remote_copy(
            src_ref=piece(kind, owner, c),
            dst_ref=piece(kind, owner, c),
            send_sem=bs_send.at[kind, way, owner],
            recv_sem=bs_recv.at[kind, owner, c],
            device_id={"fsdp": target, "dp": core},
            device_id_type=MESH,
        )

    def came(kind, owner, half):
        ref = piece(kind, owner, half)
        return pltpu.make_async_copy(ref, ref, bs_recv.at[kind, owner, half])

    def each(fn, *args):
        for kind in (0, 1):
            fn(kind, *args)

    def when(cond_, fn, *args):
        pl.when(cond_)(lambda: each(fn, *args))

    def go(kind, owner, way):
        hop(kind, owner, way).start()

    def sent(kind, owner, way):
        hop(kind, owner, way).wait_send()

    def arrive(kind, owner, half):
        came(kind, owner, half).wait()

    each(go, f, 2)
    when(z > 0, go, f, 0)
    when(z < length - 1, go, f, 1)

    def step(k, _):
        for low, way in ((True, 1), (False, 0)):
            owner = f - 2 * k if low else f + 2 * k
            there = z >= k if low else z + k < length
            onward = there & (z < length - 1 if low else z > 0)

            @pl.when(there)
            def _():
                for kind in (0, 1):
                    arrive(kind, owner, c)
                    go(kind, owner, 2)
                    go(kind, owner, 3)

            when(onward, go, owner, way)
        return _

    def from_pair(k, _):
        base = f + 1 - 2 * x
        for low in (True, False):
            owner = base - 2 * k if low else base + 2 * k
            there = z >= k if low else z + k < length

            @pl.when(there)
            def _():
                for kind in (0, 1):
                    arrive(kind, owner, c)
                    go(kind, owner, 3)
        return _

    partner = f + 1 - 2 * x
    for k in range(1, length):
        step(k, 0)
        if k == 1:
            each(arrive, partner, c)
            each(go, partner, 3)
        else:
            from_pair(k - 1, 0)
    if length > 1:
        from_pair(length - 1, 0)
    else:
        each(arrive, partner, c)
        each(go, partner, 3)

    def others(d, _):
        owner = (f + d) % nf
        each(arrive, owner, 1 - c)
        return _

    lax.fori_loop(1, nf, others, 0)
    for load in loads:
        load.wait()

    lane = lax.broadcasted_iota(jnp.int32, (1, 2 * r), 1)
    first = lane < r

    def project(source, full):
        width = source.shape[1]
        chunk = 2048 if width % 2048 == 0 else width

        def part(i, total):
            at = pl.ds(pl.multiple_of(i * chunk, chunk), chunk)
            return total + dot(source[:, at], full[at, :], 1, 0)

        both = lax.fori_loop(
            0, width // chunk, part, jnp.zeros((source.shape[0], 2 * r), F32)
        )
        return jnp.where(first, both[:tokens], both[tokens:])

    def packed(both):
        return jnp.where(first, both[:r], both[r:])

    p_out = project(grads, wout)
    p_in = project(acts, win)
    acc[0, :r, :] = packed(dot(p_in, p_in, 0, 0, HIGHEST))
    acc[0, r:, :] = packed(dot(p_out, p_out, 0, 0, HIGHEST))

    place = 0
    for b in range(bits):
        place = place + (me // (1 << b)) % 2 * (1 << (bits - 1 - b))

    def partner_of(t):
        b = bits - 1 - t
        return me + (1 - 2 * ((me // (1 << b)) % 2)) * (1 << b)

    def cov_copy(t):
        return pltpu.make_async_remote_copy(
            src_ref=acc.at[t], dst_ref=arrived.at[t], send_sem=cov_send.at[t],
            recv_sem=cov_recv.at[t], device_id=peer(partner_of(t)), device_id_type=MESH,
        )

    def code_copy(t):
        size = 1 << t
        at = pl.ds(place // size * size, size)
        return pltpu.make_async_remote_copy(
            src_ref=codes.at[at], dst_ref=codes.at[at], send_sem=g_send.at[t],
            recv_sem=g_recv.at[t], device_id=peer(partner_of(t)), device_id_type=MESH,
        )

    def code_wait(t):
        size = 1 << t
        code_copy(t).wait_send()
        sib = place // size
        sib = sib + 1 - 2 * (sib % 2)
        ref = codes.at[pl.ds(sib * size, size)]
        pltpu.make_async_copy(ref, ref, g_recv.at[t]).wait()

    for t in range(bits):
        cov_copy(t).start()
        if t == 0:
            codes[place] = packed(dot(p_in, p_out, 0, 0, HIGHEST))
            code_copy(0).start()
        cov_copy(t).wait()
        acc[t + 1] = acc[t] + arrived[t]
        if t >= 1:
            code_wait(t - 1)
            code_copy(t).start()

    samples = float(n * tokens)
    eye = (
        lax.broadcasted_iota(jnp.int32, (r, r), 0) == lax.broadcasted_iota(jnp.int32, (r, r), 1)
    )
    mats = []
    for side in (0, 1):
        for layer in (0, 1):
            a = acc[bits, side * r : (side + 1) * r, :][:, layer * r : (layer + 1) * r] / samples
            diag = jnp.where(eye, a, 0.0)
            trace = jnp.sum(jnp.sum(diag, axis=1, keepdims=True), axis=0, keepdims=True)
            mats.append(a + jnp.where(eye, 0.1 * trace / r, 0.0))
    in0, in1, out0, out1 = invert_all(mats)
    code_wait(bits - 1)

    left = jnp.concatenate([in0, in1], axis=0)
    none = jnp.zeros((r, r), F32)
    right = jnp.concatenate(
        [jnp.concatenate([out0, none], axis=1), jnp.concatenate([none, out1], axis=1)], axis=0
    )

    for e in range(n):
        mid = packed(dot(left, codes[e], 1, 0, HIGHEST))
        cond[e * r : (e + 1) * r, :] = mid
    cond[...] = dot(cond[...], right, 1, 0, HIGHEST) * scale

    half = r * r
    for k in range(r // 2):
        a = cond[pl.ds(2 * k, n, stride=r), :]
        b = cond[pl.ds(2 * k + 1, n, stride=r), :]
        flat[:, k * 2 * r : (k + 1) * 2 * r] = jnp.where(first, a, pltpu.roll(b, r, 1))
        flat[:, half + k * 2 * r : half + (k + 1) * 2 * r] = jnp.where(first, pltpu.roll(a, r, 1), b)
    whole = flat[...]
    high = whole.astype(jnp.bfloat16)
    low = (whole - high.astype(F32)).astype(jnp.bfloat16)
    scores = dot(high, queries[...], 1, 1) + dot(low, queries[...], 1, 1)
    wide = stage.shape[2]
    q = scores.shape[1]
    if q < wide:
        scores = jnp.concatenate([scores, jnp.zeros((n, wide - q), F32)], axis=1)
    stage[...] = jnp.broadcast_to(scores[:, None, :], stage.shape)

    def reverse(p):
        return int(format(p, "b").zfill(bits)[::-1], 2)

    def score_copy(p):
        return pltpu.make_async_remote_copy(
            src_ref=stage.at[p], dst_ref=landed.at[me], send_sem=s_send.at[p],
            recv_sem=s_recv.at[me], device_id=peer(reverse(p)), device_id_type=MESH,
        )

    for p in range(n):
        pl.when(place != p)(lambda p=p: score_copy(p).start())
    landed[me] = stage[place]

    each(sent, f, 2)
    when(z > 0, sent, f, 0)
    when(z < length - 1, sent, f, 1)
    for k in range(1, length):
        for low_side, way in ((True, 1), (False, 0)):
            owner = f - 2 * k if low_side else f + 2 * k
            there = z >= k if low_side else z + k < length
            onward = there & (z < length - 1 if low_side else z > 0)
            when(there, sent, owner, 2)
            when(onward, sent, owner, way)

    def other_sent(d, _):
        each(sent, (f + d) % nf, 3)
        return _

    lax.fori_loop(1, nf, other_sent, 0)
    for p in range(n):
        pl.when(place != p)(lambda p=p: score_copy(p).wait_send())

    def score_in(d, _):
        who = (me + d) % n
        ref = landed.at[who]
        pltpu.make_async_copy(ref, ref, s_recv.at[who]).wait()
        return _

    lax.fori_loop(1, n, score_in, 0)
    out_ref[...] = landed[:, 0, :q]


def solution(mesh):
    nf, nc = mesh.shape["fsdp"], mesh.shape["dp"]
    n = nf * nc
    bits = n.bit_length() - 1

    def on_device(acts, grads_out, basis_in, basis_out, query_codes):
        layers, _, length, ff = acts.shape
        width = grads_out.shape[3]
        r = basis_in.shape[2]
        q, code_width = query_codes.shape
        bf16 = jnp.bfloat16
        scale = 1.0 / math.sqrt(code_width * length)
        vmem, anywhere = pl.BlockSpec(memory_space=pltpu.VMEM), pl.BlockSpec(memory_space=pl.ANY)
        dma = pltpu.SemaphoreType.DMA
        lanes = -(-q // 128) * 128
        scores = pl.pallas_call(
            functools.partial(kernel, nf, nc, scale),
            out_shape=jax.ShapeDtypeStruct((n, q), F32),
            in_specs=[anywhere, anywhere, vmem, vmem, anywhere],
            out_specs=vmem,
            scratch_shapes=[
                pltpu.VMEM((layers * length, ff), bf16),
                pltpu.VMEM((layers * length, width), bf16),
                pltpu.VMEM((q, code_width), bf16),
                pltpu.VMEM((ff, layers * r), bf16),
                pltpu.VMEM((width, layers * r), bf16),
                pltpu.VMEM((bits + 1, 2 * r, 2 * r), F32),
                pltpu.VMEM((bits, 2 * r, 2 * r), F32),
                pltpu.VMEM((n, r, 2 * r), F32),
                pltpu.VMEM((n * r, 2 * r), F32),
                pltpu.VMEM((n, code_width), F32),
                pltpu.VMEM((n, 8, lanes), F32),
                pltpu.VMEM((n, 8, lanes), F32),
                dma((3,)),
                dma((2, 4, nf)),
                dma((2, nf, 2)),
                dma((bits,)),
                dma((bits,)),
                dma((bits,)),
                dma((bits,)),
                dma((n,)),
                dma((n,)),
            ],
            compiler_params=pltpu.CompilerParams(
                collective_id=0, has_side_effects=True, vmem_limit_bytes=56 * 1024 * 1024
            ),
        )(
            acts.reshape(layers * length, ff),
            grads_out.reshape(layers * length, width),
            basis_in,
            basis_out,
            query_codes,
        )
        return scores.reshape(1, n * q)

    rows = P(None, ("groups", "fsdp", "dp"), None, None)
    return jax.shard_map(
        on_device,
        mesh=mesh,
        in_specs=(rows, rows, P(None, "fsdp", None), P(None, "fsdp", None), P(("fsdp", "dp"), None)),
        out_specs=P(("groups", "fsdp", "dp"), None),
        check_vma=False,
    )
```

time: 368 us -> 75.7 us (0.21)
  waiting for transfers between devices: 279 us -> 0 us
  Pallas kernels: 0 us -> 70.1 us
  other arithmetic: 46.1 us -> 0 us
  matrix products: 28.9 us -> 0 us
  between operations: 13.3 us -> 0.01 us
  local copies, waits for them, and re-layouts: 0.42 us -> 5.36 us
    all_gather x3 -> x0, waiting for transfers between devices: 192 us -> none  [the longest x1 83.6 us: on_device(): lax.all_gather(query_codes, ('fsdp', 'dp'), axis=0, tiled=True)]
    psum x1 -> x0, waiting for transfers between devices: 84.9 us -> none  [on_device(): lax.psum((covariance_in, covariance_out), ('fsdp', 'dp'))]
    pallas_call x0 -> x1, Pallas kernels: none -> 70.1 us  [on_device(): pl.pallas_call(functools.partial(kernel, nf, nc, scale), out_shape=jax.Sh...]
    another operation x10 -> x0, other arithmetic: 43.5 us -> none  [the longest x6 23.7 us: damped_inverse(): factor = jnp.linalg.cholesky(averaged + ridge_term * identity_matrix)]
    dot_general x8 -> x0, matrix products: 27.8 us -> none  [the longest x1 16.5 us: inner_row_count(): lax.dot_general(left_rows, right_rows, (((1,), (1,)), ((), ())), precisio...]
    unnamed x2, local copies, waits for them, and re-layouts: 0.01 us -> 3.99 us
  transfers between devices with their start and end apart: 4 -> 0, of which waited for: 4 -> 0; matrix products, arithmetic and copies ran while one was open for 14% -> 0% of each run, Pallas kernels for 0% -> 0%
where the time goes in v1:
time: 75.7 us; the launch traced here: 75.4 us
  Pallas kernels  70.1 us (93%)
  local copies, waits for them, and re-layouts  5.36 us (7%)
    pallas_call x1, Pallas kernels, on_device(): pl.pallas_call(functools.partial(kernel, nf, nc, scale), out_shape=jax.Sh...  70.1 us
    unnamed x2, local copies, waits for them, and re-layouts  3.99 us

profile of v1, /device:TPU:0, one launch (start us, length us, event | category | flops | bytes accessed | tf_op | source)
XLA Modules:
  0.0 75.4 jit_solution(13291528252044951528)
XLA Ops:
  0.0 1.7 %copy.7.basis_out = bf16[2,512,64]{2,1,0:T(8,128)(2,1)} copy(bf16[2,512,64]{1,2,0:T(8,128)(2,1)} %param.8) | data formatting | bytes 262144 | tf_op args[3]
  1.7 2.3 %copy.6.basis_in = bf16[2,1792,64]{2,1,0:T(8,128)(2,1)} copy(bf16[2,1792,64]{1,2,0:T(8,128)(2,1)} %param.7) | data formatting | bytes 917504 | tf_op args[2]
  4.0 70.1 %shard_map.55 = f32[16,64]{1,0:T(8,128)} custom-call(bf16[256,14336]{1,0:T(8,128)(2,1)} %bitcast.2, bf16[256,4096]{1,0:T(8,128)(2,1)} %bitcast.3, bf16[2,1792,64]{2,1,0:T(8,128)(2,1)} %copy.6.basis_in, bf16[2,512,64]{2,1,0:T(8,128)(2,1)} %copy.7.basis_out, bf16[64,8192]{1,0:T(8,128)(2,1)} %query_hbm.1), custom_call_target="tpu_custom_call" | custom-call | tf_op jit(solution)/shard_map/pallas_call | solution.py:336
  74.1 1.4 %reshape.11 = f32[1,1024]{1,0:T(1,128)} reshape(f32[16,64]{1,0:T(8,128)} %shard_map.55) | data formatting | bytes 8192 | tf_op jit(solution)/shard_map/reshape | solution.py:374

commit v2 on v1

--- a/solution.py
+++ b/solution.py
@@ -39,16 +39,16 @@
 def kernel(
     nf, nc, scale,
     acts_hbm, grads_hbm, basis_in, basis_out, query_hbm, out_ref,
-    acts, grads, queries, win, wout, acc, arrived, codes, cond, flat, stage, landed,
+    acts, grads, queries, win, wout, sum_in, sum_out, acc, arrived, codes, cond, flat, stage, landed,
     load_sem, bs_send, bs_recv, cov_send, cov_recv, g_send, g_recv, s_send, s_recv,
 ):
-    f, c = lax.axis_index("fsdp"), lax.axis_index("dp")
+    f, c, g = lax.axis_index("fsdp"), lax.axis_index("dp"), lax.axis_index("groups")
     n = nf * nc
     bits = n.bit_length() - 1
     me = f * nc + c
     length = nf // 2
     z, x = f // 2, f % 2
-    r = basis_in.shape[2]
+    r = basis_in.shape[0] // 2
     tokens = acts.shape[0] // 2
 
     loads = [
@@ -68,35 +68,41 @@
         return _
 
     lax.fori_loop(1, n, greet, 0)
-
-    kinds = ((win, basis_in), (wout, basis_out))
-    for full, mine in kinds:
-        rows = mine.shape[1]
-        full[pl.ds(pl.multiple_of(f * rows, rows), rows), :] = jnp.concatenate(
-            [mine[0], mine[1]], axis=1
-        )
-    pl.semaphore_wait(barrier, n - 1)
-
-    def piece(kind, owner, half):
-        full, mine = kinds[kind]
-        rows = mine.shape[1] // 2
-        return full.at[pl.ds(pl.multiple_of((owner * 2 + half) * rows, rows), rows), :]
-
-    def hop(kind, owner, way):
-        target = (f - 2, f + 2, f + 1 - 2 * x, f)[way]
-        core = 1 - c if way == 3 else c
+    other_group = {"groups": 1 - g, "fsdp": f, "dp": c}
+    pl.semaphore_signal(barrier, inc=1, device_id=other_group, device_id_type=MESH)
+
+    kinds = ((win, basis_in, acts, sum_in), (wout, basis_out, grads, sum_out))
+    for full, mine, _, total in kinds:
+        full[f] = mine[...]
+    pl.semaphore_wait(barrier, n)
+
+    def piece(kind, owner, half, part=None):
+        full = kinds[kind][0]
+        if part is None:
+            return full.at[owner, pl.ds(pl.multiple_of(half * r, r), r), :]
+        start = pl.multiple_of(half * r + part * (r // 2), r // 2)
+        return full.at[owner, pl.ds(start, r // 2), :]
+
+    def hop(kind, owner, way, halved=False):
+        target = f + 1 - 2 * x if way == 2 else {0: f - 2, 1: f + 2}.get(way, f)
+        part = None
+        if way in (2, 5) or (way == 3 and halved):
+            part = g
+        elif way == 4:
+            part = 1 - g
+        ref = piece(kind, owner, c, part)
         return pltpu.make_async_remote_copy(
-            src_ref=piece(kind, owner, c),
-            dst_ref=piece(kind, owner, c),
+            src_ref=ref,
+            dst_ref=ref,
             send_sem=bs_send.at[kind, way, owner],
-            recv_sem=bs_recv.at[kind, owner, c],
-            device_id={"fsdp": target, "dp": core},
+            recv_sem=bs_recv.at[kind, owner, c, 0 if part is None else part],
+            device_id={
+                "groups": 1 - g if way == 5 else g,
+                "fsdp": target,
+                "dp": 1 - c if way in (3, 4) else c,
+            },
             device_id_type=MESH,
         )
-
-    def came(kind, owner, half):
-        ref = piece(kind, owner, half)
-        return pltpu.make_async_copy(ref, ref, bs_recv.at[kind, owner, half])
 
     def each(fn, *args):
         for kind in (0, 1):
@@ -105,92 +111,112 @@
     def when(cond_, fn, *args):
         pl.when(cond_)(lambda: each(fn, *args))
 
-    def go(kind, owner, way):
-        hop(kind, owner, way).start()
-
-    def sent(kind, owner, way):
-        hop(kind, owner, way).wait_send()
-
-    def arrive(kind, owner, half):
-        came(kind, owner, half).wait()
-
-    each(go, f, 2)
-    when(z > 0, go, f, 0)
-    when(z < length - 1, go, f, 1)
-
-    def step(k, _):
-        for low, way in ((True, 1), (False, 0)):
-            owner = f - 2 * k if low else f + 2 * k
-            there = z >= k if low else z + k < length
-            onward = there & (z < length - 1 if low else z > 0)
-
+    def go(kind, owner, way, halved=False):
+        hop(kind, owner, way, halved).start()
+
+    def sent(kind, owner, way, halved=False):
+        hop(kind, owner, way, halved).wait_send()
+
+    def arrive(kind, owner, half, part=None):
+        ref = piece(kind, owner, half, part)
+        sem = bs_recv.at[kind, owner, half, 0 if part is None else part]
+        pltpu.make_async_copy(ref, ref, sem).wait()
+
+    early = all(mine.shape[1] % 128 == 0 for _, mine, _, _ in kinds)
+
+    def multiply(kind, owner):
+        full, mine, source, total = kinds[kind]
+        rows = mine.shape[1]
+        start = owner * rows
+        if not isinstance(owner, int):
+            start = pl.multiple_of(start, rows)
+        total[...] += dot(source[:, pl.ds(start, rows)], full[owner], 1, 1)
+
+    def on_line(kind, owner):
+        arrive(kind, owner, 1 - c)
+        if early:
+            multiply(kind, owner)
+
+    def on_pair(kind, owner):
+        arrive(kind, owner, 1 - c, 0)
+        arrive(kind, owner, 1 - c, 1)
+        if early:
+            multiply(kind, owner)
+
+    def from_line(kind, owner):
+        arrive(kind, owner, c)
+        go(kind, owner, 2)
+        go(kind, owner, 3)
+
+    def from_pair(kind, owner):
+        arrive(kind, owner, c, g)
+        go(kind, owner, 5)
+        go(kind, owner, 3, True)
+
+    def from_group(kind, owner):
+        arrive(kind, owner, c, 1 - g)
+        go(kind, owner, 4)
+
+    def sides(fn, base, k):
+        if k == 0:
+            each(fn, base)
+        elif 0 < k < length:
+            when(z >= k, fn, base - 2 * k)
+            when(z + k < length, fn, base + 2 * k)
+
+    def onward(fn, k):
+        if k == 0:
+            when(z > 0, fn, f, 0)
+            when(z < length - 1, fn, f, 1)
+        elif k < length:
+            when((z >= k) & (z < length - 1), fn, f - 2 * k, 1)
+            when((z + k < length) & (z > 0), fn, f + 2 * k, 0)
+
+    def pass_on(k):
+        if k >= length:
+            return
+        for there, owner, way, further in (
+            (z >= k, f - 2 * k, 1, z < length - 1),
+            (z + k < length, f + 2 * k, 0, z > 0),
+        ):
             @pl.when(there)
             def _():
                 for kind in (0, 1):
                     arrive(kind, owner, c)
+                    pl.when(further)(lambda kind=kind: go(kind, owner, way))
                     go(kind, owner, 2)
                     go(kind, owner, 3)
 
-            when(onward, go, owner, way)
-        return _
-
-    def from_pair(k, _):
-        base = f + 1 - 2 * x
-        for low in (True, False):
-            owner = base - 2 * k if low else base + 2 * k
-            there = z >= k if low else z + k < length
-
-            @pl.when(there)
-            def _():
-                for kind in (0, 1):
-                    arrive(kind, owner, c)
-                    go(kind, owner, 3)
-        return _
-
     partner = f + 1 - 2 * x
-    for k in range(1, length):
-        step(k, 0)
-        if k == 1:
-            each(arrive, partner, c)
-            each(go, partner, 3)
-        else:
-            from_pair(k - 1, 0)
-    if length > 1:
-        from_pair(length - 1, 0)
-    else:
-        each(arrive, partner, c)
-        each(go, partner, 3)
-
-    def others(d, _):
-        owner = (f + d) % nf
-        each(arrive, owner, 1 - c)
-        return _
-
-    lax.fori_loop(1, nf, others, 0)
+    onward(go, 0)
+    each(go, f, 2)
+    for _, _, _, total in kinds:
+        total[...] = jnp.zeros_like(total)
     for load in loads:
         load.wait()
+    if early:
+        each(multiply, f)
+    for k in range(1, length + 3):
+        pass_on(k)
+        sides(from_pair, partner, k - 1)
+        if k >= 2:
+            sides(from_group, partner, k - 2)
+            if k > 2:
+                sides(on_line, f, k - 2)
+        if k >= 3:
+            sides(on_pair, partner, k - 3)
+    if not early:
+        for owner in range(nf):
+            each(multiply, owner)
 
     lane = lax.broadcasted_iota(jnp.int32, (1, 2 * r), 1)
     first = lane < r
 
-    def project(source, full):
-        width = source.shape[1]
-        chunk = 2048 if width % 2048 == 0 else width
-
-        def part(i, total):
-            at = pl.ds(pl.multiple_of(i * chunk, chunk), chunk)
-            return total + dot(source[:, at], full[at, :], 1, 0)
-
-        both = lax.fori_loop(
-            0, width // chunk, part, jnp.zeros((source.shape[0], 2 * r), F32)
-        )
-        return jnp.where(first, both[:tokens], both[tokens:])
-
     def packed(both):
         return jnp.where(first, both[:r], both[r:])
 
-    p_out = project(grads, wout)
-    p_in = project(acts, win)
+    p_out = jnp.where(first, sum_out[:tokens, :], sum_out[tokens:, :])
+    p_in = jnp.where(first, sum_in[:tokens, :], sum_in[tokens:, :])
     acc[0, :r, :] = packed(dot(p_in, p_in, 0, 0, HIGHEST))
     acc[0, r:, :] = packed(dot(p_out, p_out, 0, 0, HIGHEST))
 
@@ -289,22 +315,13 @@
         pl.when(place != p)(lambda p=p: score_copy(p).start())
     landed[me] = stage[place]
 
-    each(sent, f, 2)
-    when(z > 0, sent, f, 0)
-    when(z < length - 1, sent, f, 1)
-    for k in range(1, length):
-        for low_side, way in ((True, 1), (False, 0)):
-            owner = f - 2 * k if low_side else f + 2 * k
-            there = z >= k if low_side else z + k < length
-            onward = there & (z < length - 1 if low_side else z > 0)
-            when(there, sent, owner, 2)
-            when(onward, sent, owner, way)
-
-    def other_sent(d, _):
-        each(sent, (f + d) % nf, 3)
-        return _
-
-    lax.fori_loop(1, nf, other_sent, 0)
+    for k in range(length):
+        onward(sent, k)
+        sides(lambda kind, owner: sent(kind, owner, 2), f, k)
+        if k > 0:
+            sides(lambda kind, owner: sent(kind, owner, 3), f, k)
+        for way in (5, 3, 4):
+            sides(lambda kind, owner: sent(kind, owner, way, way == 3), partner, k)
     for p in range(n):
         pl.when(place != p)(lambda p=p: score_copy(p).wait_send())
 
@@ -342,8 +359,10 @@
                 pltpu.VMEM((layers * length, ff), bf16),
                 pltpu.VMEM((layers * length, width), bf16),
                 pltpu.VMEM((q, code_width), bf16),
-                pltpu.VMEM((ff, layers * r), bf16),
-                pltpu.VMEM((width, layers * r), bf16),
+                pltpu.VMEM((nf, layers * r, basis_in.shape[1]), bf16),
+                pltpu.VMEM((nf, layers * r, basis_out.shape[1]), bf16),
+                pltpu.VMEM((layers * length, layers * r), F32),
+                pltpu.VMEM((layers * length, layers * r), F32),
                 pltpu.VMEM((bits + 1, 2 * r, 2 * r), F32),
                 pltpu.VMEM((bits, 2 * r, 2 * r), F32),
                 pltpu.VMEM((n, r, 2 * r), F32),
@@ -352,8 +371,8 @@
                 pltpu.VMEM((n, 8, lanes), F32),
                 pltpu.VMEM((n, 8, lanes), F32),
                 dma((3,)),
-                dma((2, 4, nf)),
-                dma((2, nf, 2)),
+                dma((2, 6, nf)),
+                dma((2, nf, 2, 2)),
                 dma((bits,)),
                 dma((bits,)),
                 dma((bits,)),
@@ -367,8 +386,8 @@
         )(
             acts.reshape(layers * length, ff),
             grads_out.reshape(layers * length, width),
-            basis_in,
-            basis_out,
+            basis_in.transpose(0, 2, 1).reshape(layers * r, -1),
+            basis_out.transpose(0, 2, 1).reshape(layers * r, -1),
             query_codes,
         )
         return scores.reshape(1, n * q)

time: 75.7 us -> 71.8 us (0.948)
  local copies, waits for them, and re-layouts: 5.36 us -> 1.37 us
    unnamed x2 -> x0, local copies, waits for them, and re-layouts: 3.99 us -> none
where the time goes in v2:
time: 71.8 us; the launch traced here: 71.6 us
  Pallas kernels  70.2 us (98%)
  local copies, waits for them, and re-layouts  1.37 us (2%)
    pallas_call x1, Pallas kernels, on_device(): pl.pallas_call(functools.partial(kernel, nf, nc, scale), out_shape=jax.Sh...  70.2 us

profile of v2, /device:TPU:0, one launch (start us, length us, event | category | flops | bytes accessed | tf_op | source)
XLA Modules:
  0.0 71.6 jit_solution(13734343785121740242)
XLA Ops:
  0.0 70.2 %shard_map.55 = f32[16,64]{1,0:T(8,128)} custom-call(bf16[256,14336]{1,0:T(8,128)(2,1)} %bitcast.8, bf16[256,4096]{1,0:T(8,128)(2,1)} %bitcast.9, bf16[128,1792]{1,0:T(8,128)(2,1)} %bitcast.10, bf16[128,512]{1,0:T(8,128)(2,1)} %bitcast.11, bf16[64,8192]{1,0:T(8,128)(2,1)} %query_hbm.1), custom_call_target="tpu_custom_call" | custom-call | tf_op jit(solution)/shard_map/pallas_call | solution.py:353
  70.2 1.4 %reshape.19 = f32[1,1024]{1,0:T(1,128)} reshape(f32[16,64]{1,0:T(8,128)} %shard_map.55) | data formatting | bytes 8192 | tf_op jit(solution)/shard_map/reshape | solution.py:393

commit v3 on v2

--- a/solution.py
+++ b/solution.py
@@ -192,7 +192,7 @@
     each(go, f, 2)
     for _, _, _, total in kinds:
         total[...] = jnp.zeros_like(total)
-    for load in loads:
+    for load in loads[:2]:
         load.wait()
     if early:
         each(multiply, f)
@@ -228,10 +228,19 @@
         b = bits - 1 - t
         return me + (1 - 2 * ((me // (1 << b)) % 2)) * (1 << b)
 
+    own_side = pl.ds(pl.multiple_of(c * r, r), r)
+
     def cov_copy(t):
+        if t == 0:
+            src, dst, to = acc.at[0], arrived.at[0], me + 1 - 2 * c
+        elif t == bits:
+            src = acc.at[bits, own_side, :]
+            dst, to = src, me + 1 - 2 * c
+        else:
+            src, dst, to = acc.at[t, own_side, :], arrived.at[t, own_side, :], partner_of(t - 1)
         return pltpu.make_async_remote_copy(
-            src_ref=acc.at[t], dst_ref=arrived.at[t], send_sem=cov_send.at[t],
-            recv_sem=cov_recv.at[t], device_id=peer(partner_of(t)), device_id_type=MESH,
+            src_ref=src, dst_ref=dst, send_sem=cov_send.at[t],
+            recv_sem=cov_recv.at[t], device_id=peer(to), device_id_type=MESH,
         )
 
     def code_copy(t):
@@ -256,10 +265,18 @@
             codes[place] = packed(dot(p_in, p_out, 0, 0, HIGHEST))
             code_copy(0).start()
         cov_copy(t).wait()
-        acc[t + 1] = acc[t] + arrived[t]
+        if t == 0:
+            acc[1] = acc[0] + arrived[0]
+        else:
+            acc[t + 1, own_side, :] = acc[t, own_side, :] + arrived[t, own_side, :]
         if t >= 1:
             code_wait(t - 1)
             code_copy(t).start()
+
+    cov_copy(bits).start()
+    cov_copy(bits).wait_send()
+    other_side = acc.at[bits, pl.ds(pl.multiple_of((1 - c) * r, r), r), :]
+    pltpu.make_async_copy(other_side, other_side, cov_recv.at[bits]).wait()
 
     samples = float(n * tokens)
     eye = (
@@ -292,6 +309,7 @@
         b = cond[pl.ds(2 * k + 1, n, stride=r), :]
         flat[:, k * 2 * r : (k + 1) * 2 * r] = jnp.where(first, a, pltpu.roll(b, r, 1))
         flat[:, half + k * 2 * r : half + (k + 1) * 2 * r] = jnp.where(first, pltpu.roll(a, r, 1), b)
+    loads[2].wait()
     whole = flat[...]
     high = whole.astype(jnp.bfloat16)
     low = (whole - high.astype(F32)).astype(jnp.bfloat16)
@@ -373,8 +391,8 @@
                 dma((3,)),
                 dma((2, 6, nf)),
                 dma((2, nf, 2, 2)),
-                dma((bits,)),
-                dma((bits,)),
+                dma((bits + 1,)),
+                dma((bits + 1,)),
                 dma((bits,)),
                 dma((bits,)),
                 dma((n,)),

time: 71.8 us -> 70.2 us (0.978)
  Pallas kernels: 70.2 us -> 68.6 us
    pallas_call x1, Pallas kernels: 70.2 us -> 68.6 us  [on_device(): pl.pallas_call(functools.partial(kernel, nf, nc, scale), out_shape=jax.Sh...]
where the time goes in v3:
time: 70.2 us; the launch traced here: 70 us
  Pallas kernels  68.6 us (98%)
  local copies, waits for them, and re-layouts  1.37 us (2%)
    pallas_call x1, Pallas kernels, on_device(): pl.pallas_call(functools.partial(kernel, nf, nc, scale), out_shape=jax.Sh...  68.6 us

profile of v3, /device:TPU:0, one launch (start us, length us, event | category | flops | bytes accessed | tf_op | source)
XLA Modules:
  0.0 70.0 jit_solution(8130751856411131012)
XLA Ops:
  0.0 68.6 %shard_map.55 = f32[16,64]{1,0:T(8,128)} custom-call(bf16[256,14336]{1,0:T(8,128)(2,1)} %bitcast.8, bf16[256,4096]{1,0:T(8,128)(2,1)} %bitcast.9, bf16[128,1792]{1,0:T(8,128)(2,1)} %bitcast.10, bf16[128,512]{1,0:T(8,128)(2,1)} %bitcast.11, bf16[64,8192]{1,0:T(8,128)(2,1)} %query_hbm.1), custom_call_target="tpu_custom_call" | custom-call | tf_op jit(solution)/shard_map/pallas_call | solution.py:371
  68.6 1.4 %reshape.19 = f32[1,1024]{1,0:T(1,128)} reshape(f32[16,64]{1,0:T(8,128)} %shard_map.55) | data formatting | bytes 8192 | tf_op jit(solution)/shard_map/reshape | solution.py:411
